TPU v7x, 32 devices: a whole 2x2x4 slice. The times are simulated.
32 devices in a mesh: centre: 8 (over z, y), row: 4 (over x, core).
Axes of the slice: x: 2, y: 2, z: 4, core: 2. Of those that a mesh axis runs over, the one named last changes fastest.
Arguments:
- pool: bfloat16 [1024, 16384], P('centre', 'row')
- batch_index: int32 [1024], P('row'), may hold values from 0 to 16383, as said below
- targets: float32 [10, 1024], P(None, 'row'), may hold values from -6 to 6
- centres: bfloat16 [65536, 1024], P(('centre', 'row'))
- weights: float32 [10, 65536], P(None, ('centre', 'row')), may hold values from -0.0234375 to 0.0234375
- sample_index: int32 [512], P(('centre', 'row')), may hold values from 0 to 65535, as said below
- factor: float32 [512, 128], P(('centre', 'row')), may hold values from -0.5 to 0.5
Outputs:
- gradient: float32 [10, 1024], P(None, 'row')
- update: float32 [10, 512], P(None, ('centre', 'row'))
Inputs may be any that keep to these rules, and one draw needn't show every extreme that they name: `batch_index`: the entries at positions r * 256 to (r + 1) * 256 - 1 lie in r * 4096 to (r + 1) * 4096 - 1; repeats may occur. `sample_index`: all entries differ; the entries at positions k * 16 to (k + 1) * 16 - 1 lie in k * 2048 to (k + 1) * 2048 - 1.
All inputs are finite; a program needn't handle non-finite values.
Results may differ from a plain program's by a relative error of at most 0.0003.
Values may be sent and summed in bfloat16 or wider, within the bound.
A program may use at most 128 MiB of HBM per device.

v0:
```python
import math

import jax
import jax.numpy as jnp
from jax import lax
from jax.sharding import PartitionSpec as P

PROJ_STEPS = 2


EPS = 1e-06
HIGH = lax.Precision.HIGHEST


def row_scale(rows, axis):
    values = rows.astype(jnp.float32)
    return jnp.sqrt(jnp.mean(values * values, axis=axis) + EPS)


def tangent_kernel(inner, left_scale, right_scale, width):
    product = left_scale[:, None] * right_scale[None, :]
    cosine = jnp.clip(inner / (width * product), -1.0, 1.0)
    angle = jnp.arccos(cosine)
    first = (math.pi - angle) / math.pi
    second = (cosine * (math.pi - angle) + jnp.sqrt(1.0 - cosine * cosine)) / math.pi
    return product * (second + cosine * first)


def on_device(pool, batch_index, targets, centres, weights, sample_index, factor):
    width = float(centres.shape[1])
    labels = weights.shape[0]
    rows_dev = batch_index.shape[0]
    pool_dev = pool.shape[1]
    cent_dev = centres.shape[0]
    samp_dev = sample_index.shape[0]
    row_count = lax.axis_size("row")
    total_rows = rows_dev * row_count
    total_samp = samp_dev * row_count * lax.axis_size("centre")
    contract = (((1,), (1,)), ((), ()))
    local_batch = batch_index - lax.axis_index("row") * pool_dev
    picked = jnp.take(pool, local_batch, axis=1)
    features = lax.all_gather(picked, "centre", axis=0, tiled=True)
    all_targets = lax.all_gather(targets, "row", axis=1, tiled=True)
    centre_scale = row_scale(centres, 1)
    local_sample = sample_index - lax.axis_index(("centre", "row")) * cent_dev
    sample_rows = jnp.take(centres, local_sample, axis=0)
    sample_scale = jnp.take(centre_scale, local_sample)
    piece = lax.all_gather(features, "row", axis=1, tiled=True)
    inner = jnp.dot(centres, piece, preferred_element_type=jnp.float32)
    kernel = tangent_kernel(inner, centre_scale, row_scale(piece, 0), width)
    partial_value = jnp.dot(weights, kernel, precision=HIGH)
    tiles = jnp.concatenate([partial_value, jnp.take(kernel, local_sample, axis=0)], axis=0)
    partial_value = tiles[:labels]
    cross = tiles[labels:]
    totals = lax.psum(partial_value, ("centre", "row"))
    gradient_all = totals - all_targets
    gradient = lax.dynamic_slice_in_dim(gradient_all, lax.axis_index("row") * rows_dev, rows_dev, 1)
    push = lax.dot_general(gradient_all, cross, contract, precision=HIGH) / total_rows
    piece = lax.all_gather(sample_rows, ("centre", "row"), axis=0, tiled=True)
    inner = lax.dot_general(sample_rows, piece, contract, preferred_element_type=jnp.float32)
    block = tangent_kernel(inner, sample_scale, row_scale(piece, 1), width)
    update = jnp.zeros((labels, samp_dev), jnp.float32)
    for step in range(PROJ_STEPS):
        if step == 0:
            slope = push
        else:
            update_whole = lax.all_gather(update, ("centre", "row"), axis=1, tiled=True)
            slope = (
                lax.dot_general(update_whole, block, contract, precision=HIGH) / total_samp + push
            )
        coef = lax.psum(jnp.dot(slope, factor, precision=HIGH), ("centre", "row"))
        update = update - (slope - jnp.dot(coef, factor.T, precision=HIGH))
    return (gradient, update)


def solution(mesh):
    placed = (
        P("centre", "row"),
        P("row"),
        P(None, "row"),
        P(("centre", "row"), None),
        P(None, ("centre", "row")),
        P(("centre", "row")),
        P(("centre", "row"), None),
    )
    return jax.shard_map(
        on_device,
        mesh=mesh,
        in_specs=placed,
        out_specs=(P(None, "row"), P(None, ("centre", "row"))),
        check_vma=False,
    )
```

profile of v0, /device:TPU:0, one launch (start us, length us, event | category | flops | bytes accessed | tf_op | source)
XLA Modules:
  0.0 313.9 jit_solution(3120540883913514165)
XLA Ops:
  7.2 0.7 compare_and_fusion
  7.9 3.3 %gather_fusion.3 = bf16[16,1024]{1,0:T(8,128)(2,1)S(1)} fusion(bf16[2048,1024]{1,0:T(8,128)(2,1)} %param.10, s32[1024]{0:T(1024)S(1)} %pad_clamp_fusion), kind=kCustom, calls=%fused_computation.3 | custom fusion | bytes 65600 | tf_op jit(solution)/shard_map/jit(_take)/gather | solution.py:46
  11.3 0.7 broadcast_select_fusion
  12.0 1.6 copy.13
  13.6 0.7 compare_and_fusion.1
  14.3 0.9 gather_fusion
  15.3 31.1 %all_gather.15 = bf16[1024,256]{0,1:T(8,128)(2,1)} all-gather(bf16[128,256]{0,1:T(8,128)(2,1)S(1)} %select_bitcast_fusion), channel_id=1, replica_groups=mesh['centre'=8,'row'=4] {'centre'}, dimensions={0}, use_global_device_ids=true | all-gather | bytes 589824 | tf_op jit(solution)/shard_map/all_gather | solution.py:42
  46.4 3.1 multiply_reduce_fusion
  49.5 0.7 gather_fusion.2
  50.2 5.2 %all_gather.17 = f32[10,1024]{1,0:T(8,128)S(1)} all-gather(f32[10,256]{1,0:T(8,128)S(1)} %copy-done.3), channel_id=1, replica_groups=mesh['centre'=8,'row'=4] {'row'}, dimensions={1}, use_global_device_ids=true | all-gather | bytes 51200 | tf_op jit(solution)/shard_map/all_gather | solution.py:43
  55.4 13.2 %all-gather.5.cloned.1.call-done = bf16[512,1024]{1,0:T(8,128)(2,1)} async-done(((bf16[16,1024]{1,0:T(8,128)(2,1)}), bf16[512,1024]{1,0:T(8,128)(2,1)}) %all-gather.5.cloned.1.call-update) | async-done | bytes 1048592 | tf_op jit(solution)/shard_map/all_gather | solution.py:59
  68.6 1.5 multiply_reduce_fusion.2
  70.1 1.6 fusion.2
  71.7 20.0 %all-gather.3.cloned.1.call-done = bf16[1024,1024]{0,1:T(8,128)(2,1)} async-done(((bf16[1024,256]{0,1:T(8,128)(2,1)}), bf16[1024,1024]{0,1:T(8,128)(2,1)}) %all-gather.3.cloned.1.call-update) | async-done | bytes 2097168 | tf_op jit(solution)/shard_map/all_gather | solution.py:48
  91.7 2.1 multiply_reduce_fusion.1
  93.8 29.3 %multiply_multiply_fusion = f32[2048,1024]{0,1:T(8,128)} fusion(bf16[1024,1024]{0,1:T(8,128)(2,1)} %all-gather.3.cloned.1.call-done, bf16[2048,1024]{1,0:T(8,128)(2,1)} %param.10, f32[1024]{0:T(1024)S(1)} %add_sqrt_fusion.1, f32[2048]{0:T(1024)S(1)} %add_sqrt_fusion), kind=kOutput, calls=%fused_computation.4 | convolution fusion | flops 4330618880 | bytes 14692352 | tf_op jit(solution)/shard_map/dot_general | solution.py:49
  123.1 9.3 %copy.14 = f32[2048,1024]{1,0:T(8,128)} copy(f32[2048,1024]{0,1:T(8,128)} %multiply_multiply_fusion) | data formatting | bytes 16777216 | tf_op jit(solution)/shard_map/mul | solution.py:26
  132.4 4.0 %gather_fusion.1 = f32[16,1024]{1,0:T(8,128)S(1)} fusion(f32[2048,1024]{1,0:T(8,128)} %copy.14, s32[1024]{0:T(1024)S(1)} %pad_clamp_fusion), kind=kCustom, calls=%fused_computation.1 | custom fusion | bytes 131136 | tf_op jit(solution)/shard_map/jit(_take)/gather | solution.py:52
  136.4 9.4 %convolution_bitcast_fusion = f32[10,1024]{1,0:T(8,128)S(1)} fusion(f32[2048,1024]{0,1:T(8,128)} %multiply_multiply_fusion, f32[10,2048]{1,0:T(8,128)S(1)} %copy-done), kind=kOutput, calls=%fused_computation.11 | convolution fusion | flops 251658240 | bytes 8511488 | tf_op jit(solution)/shard_map/dot_general | solution.py:51
  145.9 39.6 %psum.21 = f32[10,1024]{1,0:T(8,128)S(1)} all-reduce(f32[10,1024]{1,0:T(8,128)S(1)} %convolution_bitcast_fusion), channel_id=1, replica_groups=mesh['centre'=8,'row'=4] {'centre','row'}, use_global_device_ids=true, to_apply=%region_2.3 | all-reduce | flops 10240 | bytes 81920 | tf_op jit(solution)/shard_map/psum | solution.py:55
  185.9 41.0 %psum.22 = f32[10,128]{1,0:T(8,128)S(1)} all-reduce(f32[10,128]{1,0:T(8,128)S(1)} %fusion.33), channel_id=1, replica_groups=mesh['centre'=8,'row'=4] {'centre','row'}, use_global_device_ids=true, to_apply=%region_3.4 | all-reduce | flops 1280 | bytes 10240 | tf_op jit(solution)/shard_map/psum | solution.py:71
  227.1 41.0 %all_gather.18 = f32[10,512]{0,1:T(8,128)S(1)} all-gather(f32[10,16]{0,1:T(8,128)S(1)} %copy.15), channel_id=1, replica_groups=mesh['centre'=8,'row'=4] {'centre','row'}, dimensions={1}, use_global_device_ids=true | all-gather | bytes 21120 | tf_op jit(solution)/shard_map/all_gather | solution.py:67
  268.8 36.9 %psum.23 = f32[10,128]{1,0:T(8,128)S(1)} all-reduce(f32[10,128]{1,0:T(8,128)S(1)} %fusion.34), channel_id=1, replica_groups=mesh['centre'=8,'row'=4] {'centre','row'}, use_global_device_ids=true, to_apply=%region_5.6 | all-reduce | flops 1280 | bytes 10240 | tf_op jit(solution)/shard_map/psum | solution.py:71
  305.7 0.7 fusion.3
  (27 shorter events, 2.2 us)
Async XLA Ops:
  7.2 129.3 %copy-start = (f32[10,2048]{1,0:T(8,128)S(1)}, f32[10,2048]{1,0:T(8,128)}, u32[]{:S(2)}) copy-start(f32[10,2048]{1,0:T(8,128)} %param.11) | copy-start | bytes 245764
  7.2 43.0 %copy-start.3 = (f32[10,256]{1,0:T(8,128)S(1)}, f32[10,256]{1,0:T(8,128)}, u32[]{:S(2)}) copy-start(f32[10,256]{1,0:T(8,128)} %param.9) | copy-start | bytes 30724
  7.2 61.4 %all-gather.5.cloned.1.call-start = ((), (), s32[]{:S(2)}) async-start(), calls=%async_computation.1 | async-start | bytes 1081344 | tf_op jit(solution)/shard_map/all_gather | solution.py:59
  11.9 58.2 %copy-start.1 = (bf16[16,1024]{1,0:T(8,128)(2,1)S(1)}, bf16[16,1024]{1,0:T(8,128)(2,1)}, u32[]{:S(2)}) copy-start(bf16[16,1024]{1,0:T(8,128)(2,1)} %broadcast_select_fusion) | copy-start | bytes 98308
  12.0 79.8 %all-gather.3.cloned.1.call-start = ((), (), s32[]{:S(2)}) async-start(), calls=%async_computation | async-start | bytes 2621440 | tf_op jit(solution)/shard_map/all_gather | solution.py:48
  132.4 53.3 %copy-start.2 = (f32[16,128]{1,0:T(8,128)S(1)}, f32[16,128]{1,0:T(8,128)}, u32[]{:S(2)}) copy-start(f32[16,128]{1,0:T(8,128)} %param.13) | copy-start | bytes 24580
Sparse Core Ops, SparseCore 0:
  12.1 56.4 all-gather.4
  70.1 21.5 all-gather.2
where the time goes:
time: 315 us; the launch traced here: 314 us
  blocking collectives  195 us (62%)
  matrix products  42.3 us (13%)
  waiting for transfers between devices  33.2 us (11%)
  local copies, waits for them, and re-layouts  20.5 us (7%)
  between operations  14.2 us (5%)
  other arithmetic  8.84 us (3%)
    psum x2, blocking collectives, on_device(): coef = lax.psum(jnp.dot(slope, factor, precision=HIGH), ('centre', 'row'))  77.9 us
    all_gather x1, blocking collectives, on_device(): update_whole = lax.all_gather(update, ('centre', 'row'), axis=1, tiled=True)  41 us
    psum x1, blocking collectives, on_device(): totals = lax.psum(partial_value, ('centre', 'row'))  39.6 us
    all_gather x1, blocking collectives, on_device(): features = lax.all_gather(picked, 'centre', axis=0, tiled=True)  31.1 us
    dot_general x1, matrix products, on_device(): inner = jnp.dot(centres, piece, preferred_element_type=jnp.float32)  29.3 us
    all_gather x1, waiting for transfers between devices, on_device(): piece = lax.all_gather(features, 'row', axis=1, tiled=True)  20 us
    all_gather x1, waiting for transfers between devices, on_device(): piece = lax.all_gather(sample_rows, ('centre', 'row'), axis=0, tiled=True)  13.2 us
    dot_general x1, matrix products, on_device(): partial_value = jnp.dot(weights, kernel, precision=HIGH)  9.43 us
  transfers between devices with their start and end apart: 2, of which 2 were waited for; matrix products, arithmetic and copies ran while one was open for 3% of the time, Pallas kernels for 0%

commit v1 on v0

v1 whole, which is shorter than its diff:
```python
import functools
import math

import jax
import jax.numpy as jnp
from jax import lax
from jax.experimental import pallas as pl
from jax.experimental.pallas import tpu as pltpu
from jax.sharding import PartitionSpec as P

PROJ_STEPS = 2
EPS = 1e-06
HIGH = lax.Precision.HIGHEST
MESH = pl.DeviceIdType.MESH
CONTRACT = (((1,), (1,)), ((), ()))
VMEM = pl.BlockSpec(memory_space=pltpu.VMEM)
POLY = (0.3183098802, -0.8408441305, 0.09680761083, -0.03656900053,
        0.01880055716, -0.00968401399, 0.003746990699, -0.0007261497719)


def row_scale(rows, axis):
    values = rows.astype(jnp.float32)
    return jnp.sqrt(jnp.mean(values * values, axis=axis) + EPS)


def arc(cosine):
    size = jnp.minimum(jnp.abs(cosine), 1.0)
    rest = 1.0 - size
    root = rest * lax.rsqrt(jnp.maximum(rest, 1e-30))
    value = jnp.full_like(size, POLY[-1])
    for factor in POLY[-2::-1]:
        value = value * size + factor
    linear = jnp.minimum(jnp.maximum(cosine, 0.0), 1.0)
    return root * value + (linear + linear)


def pick_kernel(pool_ref, index_ref, out_ref):
    count = index_ref.shape[1]
    depth = pool_ref.shape[1]
    tile = 512
    total = jnp.zeros(out_ref.shape, jnp.float32)
    for start in range(0, depth, tile):
        size = min(tile, depth - start)
        wanted = index_ref[...] - start
        hot = lax.broadcasted_iota(jnp.int32, (size, count), 0) == wanted
        total += jnp.dot(pool_ref[:, start:start + size], hot.astype(jnp.bfloat16),
                         preferred_element_type=jnp.float32)
    out_ref[...] = total.astype(out_ref.dtype)


def gather_kernel(groups, rows, count, *refs):
    ins, outs = refs[:count], refs[count:2 * count]
    (own, send1, recv1, send2, recv2, send3, recv3) = refs[2 * count:]
    pairs = rows // 2
    c = lax.axis_index("centre")
    r = lax.axis_index("row")
    x, core = r // 2, r % 2
    other = r + 1 - 2 * core

    barrier = pltpu.get_barrier_semaphore()
    for d in range(1, groups):
        pl.semaphore_signal(barrier, inc=1, device_id=((c + d) % groups, r), device_id_type=MESH)
    for d in range(1, pairs):
        pl.semaphore_signal(barrier, inc=1, device_id=(c, ((x + d) % pairs) * 2 + core), device_id_type=MESH)
    pl.semaphore_signal(barrier, inc=1, device_id=(c, other), device_id_type=MESH)
    pl.semaphore_wait(barrier, groups - 1 + pairs - 1 + 1)

    def slot(a, row, centre):
        size = ins[a].shape[0]
        return outs[a].at[row, pl.ds(pl.multiple_of(centre * size, size), size), :]

    sent = []
    for a in range(count):
        for d in range(1, groups):
            to = (c + d) % groups
            copy = pltpu.make_async_remote_copy(
                ins[a], slot(a, r, c), send1.at[a, d], recv1.at[a, d],
                device_id=(to, r), device_id_type=MESH)
            copy.start()
            sent.append(copy)
    keep = []
    for a in range(count):
        copy = pltpu.make_async_copy(ins[a], slot(a, r, c), own.at[a])
        copy.start()
        keep.append(copy)
    for copy in keep:
        copy.wait()

    def forward(a, row, d, x_step):
        place = slot(a, row, (c + groups - d) % groups)
        copy = pltpu.make_async_remote_copy(
            place, place, send3.at[a, x_step, d], recv3.at[a, x_step, d],
            device_id=(c, other), device_id_type=MESH)
        copy.start()
        sent.append(copy)

    for a in range(count):
        for d in range(groups):
            place = slot(a, r, (c + groups - d) % groups)
            if d:
                pltpu.make_async_remote_copy(
                    ins[a], place, send1.at[a, d], recv1.at[a, d],
                    device_id=(c, r), device_id_type=MESH).wait_recv()
            for e in range(1, pairs):
                copy = pltpu.make_async_remote_copy(
                    place, place, send2.at[a, e, d], recv2.at[a, e, d],
                    device_id=(c, ((x + e) % pairs) * 2 + core), device_id_type=MESH)
                copy.start()
                sent.append(copy)
            forward(a, r, d, 0)
    for a in range(count):
        for d in range(groups):
            for e in range(1, pairs):
                row = ((x + pairs - e) % pairs) * 2 + core
                place = slot(a, row, (c + groups - d) % groups)
                pltpu.make_async_remote_copy(
                    place, place, send2.at[a, e, d], recv2.at[a, e, d],
                    device_id=(c, r), device_id_type=MESH).wait_recv()
                forward(a, row, d, e)
    for a in range(count):
        for d in range(groups):
            for e in range(pairs):
                row = ((x + pairs - e) % pairs) * 2 + (1 - core)
                place = slot(a, row, (c + groups - d) % groups)
                pltpu.make_async_remote_copy(
                    place, place, send3.at[a, e, d], recv3.at[a, e, d],
                    device_id=(c, r), device_id_type=MESH).wait_recv()
    for copy in sent:
        copy.wait_send()


def gather_all(groups, rows, arrays):
    count = len(arrays)
    pairs = rows // 2
    dma = pltpu.SemaphoreType.DMA
    return pl.pallas_call(
        functools.partial(gather_kernel, groups, rows, count),
        out_shape=[jax.ShapeDtypeStruct((rows, groups * a.shape[0], a.shape[1]), a.dtype) for a in arrays],
        in_specs=[VMEM] * count,
        out_specs=[VMEM] * count,
        scratch_shapes=[
            dma((count,)),
            dma((count, groups)), dma((count, groups)),
            dma((count, pairs, groups)), dma((count, pairs, groups)),
            dma((count, pairs, groups)), dma((count, pairs, groups)),
        ],
        compiler_params=pltpu.CompilerParams(
            collective_id=0, has_side_effects=True, vmem_limit_bytes=48 << 20),
    )(*arrays)


def main_kernel(tile, cent_ref, inv_ref, weight_ref, batch_ref, bscale_ref, samp_ref, sinv_ref, sscale_ref,
                part_ref, cross_ref):
    bscale = bscale_ref[0]
    binv = 1.0 / bscale
    batch = batch_ref[0]
    half = weight_ref.shape[0]
    first = jnp.zeros((2 * half, batch.shape[1]), jnp.float32)
    second = jnp.zeros((half, batch.shape[1]), jnp.float32)
    for start in range(0, cent_ref.shape[0], tile):
        inner = jnp.dot(cent_ref[start:start + tile, :], batch, preferred_element_type=jnp.float32)
        value = arc(inner * inv_ref[start:start + tile, :] * binv)
        high = value.astype(jnp.bfloat16)
        low = (value - high.astype(jnp.float32)).astype(jnp.bfloat16)
        exact = weight_ref[:, start:start + tile]
        upper = exact.astype(jnp.bfloat16)
        lower = (exact - upper.astype(jnp.float32)).astype(jnp.bfloat16)
        coeffs = jnp.concatenate([upper, lower], axis=0)
        first += jnp.dot(coeffs, high, preferred_element_type=jnp.float32)
        second += jnp.dot(upper, low, preferred_element_type=jnp.float32)
    part_ref[0] = (first[:half] + (first[half:] + second)) * bscale
    count = samp_ref.shape[0]
    step = min(tile, count)
    for start in range(0, count, step):
        inner = jnp.dot(samp_ref[start:start + step, :], batch, preferred_element_type=jnp.float32)
        value = arc(inner * sinv_ref[start:start + step, :] * binv)
        cross_ref[0, start:start + step, :] = value * (sscale_ref[start:start + step, :] * bscale)


def gram_kernel(left_ref, linv_ref, lscale_ref, right_ref, rscale_ref, out_ref):
    inner = lax.dot_general(left_ref[...], right_ref[...], CONTRACT, preferred_element_type=jnp.float32)
    rscale = rscale_ref[...]
    value = arc(inner * linv_ref[...] * (1.0 / rscale))
    out_ref[...] = value * (lscale_ref[...] * rscale)


def sum_kernel(groups, rows, part_ref, target_ref, grad_ref, all_ref, buf1, buf2, mine,
               send1, recv1, send2, recv2, send3, recv3):
    c = lax.axis_index("centre")
    r = lax.axis_index("row")
    barrier = pltpu.get_barrier_semaphore()
    for d in range(1, rows):
        pl.semaphore_signal(barrier, inc=1, device_id=(c, (r + d) % rows), device_id_type=MESH)
    for d in range(1, groups):
        pl.semaphore_signal(barrier, inc=1, device_id=((c + d) % groups, r), device_id_type=MESH)
    pl.semaphore_wait(barrier, rows - 1 + groups - 1)
    sent = []

    def move(src, dst, send, recv, to):
        copy = pltpu.make_async_remote_copy(src, dst, send, recv, device_id=to, device_id_type=MESH)
        copy.start()
        sent.append(copy)

    def landed(dst, send, recv):
        pltpu.make_async_remote_copy(dst, dst, send, recv, device_id=(c, r), device_id_type=MESH).wait_recv()

    for d in range(1, rows):
        to = (r + d) % rows
        move(part_ref.at[to], buf1.at[d], send1.at[d], recv1.at[d], (c, to))
    total = part_ref[r]
    for d in range(1, rows):
        landed(buf1.at[d], send1.at[d], recv1.at[d])
        total += buf1[d]
    mine[...] = total
    for d in range(1, groups):
        move(mine, buf2.at[c], send2.at[d], recv2.at[d], ((c + d) % groups, r))
    for d in range(1, groups):
        place = buf2.at[(c + groups - d) % groups]
        landed(place, send2.at[d], recv2.at[d])
    buf2[c] = total
    total = buf2[0]
    for d in range(1, groups):
        total += buf2[d]
    grad = total - target_ref[...]
    grad_ref[...] = grad
    all_ref[r] = grad
    for d in range(1, rows):
        move(grad_ref, all_ref.at[r], send3.at[d], recv3.at[d], (c, (r + d) % rows))
    for d in range(1, rows):
        landed(all_ref.at[(r + rows - d) % rows], send3.at[d], recv3.at[d])
    for copy in sent:
        copy.wait_send()


def on_device(pool, batch_index, targets, centres, weights, sample_index, factor):
    width = float(centres.shape[1])
    labels = weights.shape[0]
    rows_dev = batch_index.shape[0]
    pool_dev = pool.shape[1]
    cent_dev = centres.shape[0]
    samp_dev = sample_index.shape[0]
    rows = lax.axis_size("row")
    groups = lax.axis_size("centre")
    total_rows = rows_dev * rows
    total_samp = samp_dev * rows * groups
    whole = total_samp <= 1024
    half = -(-labels // 16) * 16
    params = pltpu.CompilerParams(vmem_limit_bytes=48 << 20)

    local_batch = batch_index - lax.axis_index("row") * pool_dev
    picked = pl.pallas_call(
        pick_kernel,
        out_shape=jax.ShapeDtypeStruct((pool.shape[0], rows_dev), pool.dtype),
        compiler_params=params,
    )(pool, local_batch[None, :])
    local_sample = sample_index - lax.axis_index(("centre", "row")) * cent_dev
    sample_rows = jnp.take(centres, local_sample, axis=0)
    arrays = [picked, sample_rows] + ([factor] if whole else [])
    gathered = gather_all(groups, rows, arrays)
    batch = gathered[0]
    samples = gathered[1].reshape(total_samp, -1)

    centre_scale = row_scale(centres, 1)
    scaled = jnp.pad(weights * centre_scale[None, :], ((0, half - labels), (0, 0)))
    inv = (1.0 / (width * centre_scale))[:, None]
    bscale = row_scale(batch, 1)[:, None, :]
    sscale = row_scale(samples, 1)
    left = samples if whole else sample_rows
    lscale = (sscale if whole else row_scale(sample_rows, 1))[:, None]
    linv = 1.0 / (width * lscale)
    extra = left.shape[0]
    fixed = lambda shape: pl.BlockSpec(shape, lambda i: (0, 0))
    moving = lambda a, b: pl.BlockSpec((1, a, b), lambda i: (i, 0, 0))
    partial, cross = pl.pallas_call(
        functools.partial(main_kernel, 256),
        grid=(rows,),
        out_shape=[jax.ShapeDtypeStruct((rows, half, rows_dev), jnp.float32),
                   jax.ShapeDtypeStruct((rows, extra, rows_dev), jnp.float32)],
        in_specs=[fixed(centres.shape), fixed(inv.shape), fixed(scaled.shape),
                  moving(batch.shape[1], rows_dev), moving(1, rows_dev),
                  fixed(left.shape), fixed(linv.shape), fixed(lscale.shape)],
        out_specs=[moving(half, rows_dev), moving(extra, rows_dev)],
        compiler_params=params,
    )(centres, inv, scaled, batch, bscale, left, linv, lscale)
    tile = min(512, total_samp)
    gram = pl.pallas_call(
        gram_kernel,
        grid=(total_samp // tile,),
        out_shape=jax.ShapeDtypeStruct((extra, total_samp), jnp.float32),
        in_specs=[fixed(left.shape), fixed(linv.shape), fixed(lscale.shape),
                  pl.BlockSpec((tile, samples.shape[1]), lambda i: (i, 0)),
                  pl.BlockSpec((1, tile), lambda i: (0, i))],
        out_specs=pl.BlockSpec((extra, tile), lambda i: (0, i)),
        compiler_params=params,
    )(left, linv, lscale, samples, sscale[None, :])

    dma = pltpu.SemaphoreType.DMA
    block = (half, rows_dev)
    grad, grad_all = pl.pallas_call(
        functools.partial(sum_kernel, groups, rows),
        out_shape=[jax.ShapeDtypeStruct(block, jnp.float32),
                   jax.ShapeDtypeStruct((rows,) + block, jnp.float32)],
        in_specs=[VMEM, VMEM],
        out_specs=[VMEM, VMEM],
        scratch_shapes=[
            pltpu.VMEM((rows,) + block, jnp.float32),
            pltpu.VMEM((groups,) + block, jnp.float32),
            pltpu.VMEM(block, jnp.float32),
            dma((rows,)), dma((rows,)), dma((groups,)), dma((groups,)), dma((rows,)), dma((rows,)),
        ],
        compiler_params=pltpu.CompilerParams(
            collective_id=1, has_side_effects=True, vmem_limit_bytes=48 << 20),
    )(partial, jnp.pad(targets, ((0, half - labels), (0, 0))))
    gradient = grad[:labels]

    def times(a, b):
        return jnp.dot(a, b, precision=HIGH)

    push = sum(lax.dot_general(grad_all[i], cross[i], CONTRACT, precision=HIGH) for i in range(rows)) / total_rows
    if whole:
        factors = gathered[2].reshape(total_samp, -1)
        update = jnp.zeros_like(push)
        for step in range(PROJ_STEPS):
            slope = push if step == 0 else times(update, gram) / total_samp + push
            coef = times(slope, factors)
            update = update - (slope - lax.dot_general(coef, factors, CONTRACT, precision=HIGH))
        place = (lax.axis_index("row") * groups + lax.axis_index("centre")) * samp_dev
        return (gradient, lax.dynamic_slice(update, (0, place), (half, samp_dev))[:labels])
    push = push[:labels]
    update = jnp.zeros((labels, samp_dev), jnp.float32)
    for step in range(PROJ_STEPS):
        if step == 0:
            slope = push
        else:
            update_whole = lax.all_gather(update, ("row", "centre"), axis=1, tiled=True)
            slope = lax.dot_general(update_whole, gram, CONTRACT, precision=HIGH) / total_samp + push
        coef = lax.psum(times(slope, factor), ("centre", "row"))
        update = update - (slope - times(coef, factor.T))
    return (gradient, update)


def solution(mesh):
    placed = (
        P("centre", "row"),
        P("row"),
        P(None, "row"),
        P(("centre", "row"), None),
        P(None, ("centre", "row")),
        P(("centre", "row")),
        P(("centre", "row"), None),
    )
    return jax.shard_map(
        on_device,
        mesh=mesh,
        in_specs=placed,
        out_specs=(P(None, "row"), P(None, ("centre", "row"))),
        check_vma=False,
    )
```

time: 315 us -> 90.9 us (0.29)
  blocking collectives: 195 us -> 0 us
  Pallas kernels: 0 us -> 69.6 us
  matrix products: 42.3 us -> 3.85 us
  waiting for transfers between devices: 33.2 us -> 0 us
  between operations: 14.2 us -> 0.86 us
  local copies, waits for them, and re-layouts: 20.5 us -> 8.06 us
    psum x3 -> x0, blocking collectives: 118 us -> none  [the longest x2 77.9 us: on_device(): coef = lax.psum(jnp.dot(slope, factor, precision=HIGH), ('centre', 'row'))]
    all_gather x3 -> x0, blocking collectives: 77.3 us -> none  [the longest x1 41 us: on_device(): update_whole = lax.all_gather(update, ('centre', 'row'), axis=1, tiled=True)]
    pallas_call x0 -> x5, Pallas kernels: none -> 69.6 us  [the longest x1 32.8 us: gather_all(): pl.pallas_call(functools.partial(gather_kernel, groups, rows, count), out...]
    dot_general x9, matrix products: 42.3 us -> 3.85 us  [the longest x4 2.11 us: on_device(): lax.dot_general(grad_all[i], cross[i], CONTRACT, precision=HIGH)]
    all_gather x2 -> x0, waiting for transfers between devices: 33.2 us -> none  [the longest x1 20 us: on_device(): piece = lax.all_gather(features, 'row', axis=1, tiled=True)]
    mul x1 -> x0, local copies, waits for them, and re-layouts: 9.27 us -> none  [tangent_kernel(): return product * (second + cosine * first)]
    gather x3 -> x0, local copies, waits for them, and re-layouts: 5.51 us -> none  [the longest x1 4 us: on_device(): jnp.take(kernel, local_sample, axis=0)]
  transfers between devices with their start and end apart: 2 -> 0, of which waited for: 2 -> 0; matrix products, arithmetic and copies ran while one was open for 3% -> 0% of each run, Pallas kernels for 0% -> 0%
where the time goes in v1:
time: 90.9 us; the launch traced here: 90.5 us
  Pallas kernels  69.6 us (77%)
  other arithmetic  8.23 us (9%)
  local copies, waits for them, and re-layouts  8.06 us (9%)
  matrix products  3.85 us (4%)
    pallas_call x1, Pallas kernels, gather_all(): pl.pallas_call(functools.partial(gather_kernel, groups, rows, count), out...  32.8 us
    pallas_call x1, Pallas kernels, on_device(): pl.pallas_call(functools.partial(main_kernel, 256), grid=(rows,), out_sha...  18.5 us
    pallas_call x1, Pallas kernels, on_device(): pl.pallas_call(functools.partial(sum_kernel, groups, rows), out_shape=[ja...  16.2 us
    unnamed x17, local copies, waits for them, and re-layouts  4.18 us
    reduce_sum x3, other arithmetic, row_scale(): return jnp.sqrt(jnp.mean(values * values, axis=axis) + EPS)  3.81 us
    gather x1, local copies, waits for them, and re-layouts, on_device(): sample_rows = jnp.take(centres, local_sample, axis=0)  3.34 us
    dot_general x4, matrix products, on_device(): lax.dot_general(grad_all[i], cross[i], CONTRACT, precision=HIGH)  2.11 us

profile of v1, /device:TPU:0, one launch (start us, length us, event | category | flops | bytes accessed | tf_op | source)
XLA Modules:
  0.0 90.5 jit_solution(6429717795395219206)
XLA Ops:
  0.6 0.7 compare_and_fusion
  1.3 3.3 %gather_fusion = bf16[16,1024]{1,0:T(8,128)(2,1)S(1)} fusion(bf16[2048,1024]{1,0:T(8,128)(2,1)} %cent_ref.1, s32[1024]{0:T(1024)S(1)} %pad_clamp_fusion), kind=kCustom, calls=%fused_computation | custom fusion | bytes 65600 | tf_op jit(solution)/shard_map/jit(_take)/gather | solution.py:257
  4.7 0.7 broadcast_subtract_fusion
  5.4 1.2 %copy-done.4 = bf16[128,4096]{1,0:T(8,128)(2,1)S(1)} copy-done((bf16[128,4096]{1,0:T(8,128)(2,1)S(1)}, bf16[128,4096]{1,0:T(8,128)(2,1)}, u32[]{:S(2)}) %copy-start.4) | copy-done | bytes 1048600
  6.6 0.4 shard_map.86.refs_0_
  7.1 0.7 copy-done.5
  7.8 32.8 %shard_map.87 = (bf16[4,1024,256]{2,1,0:T(8,128)(2,1)S(1)}, bf16[4,128,1024]{2,1,0:T(8,128)(2,1)S(1)}, f32[4,128,128]{2,1,0:T(8,128)S(1)}) custom-call(bf16[128,256]{1,0:T(8,128)(2,1)S(1)} %shard_map.86.refs_0_, bf16[16,1024]{1,0:T(8,128)(2,1)S(1)} %broadcast_select_fusion.refs_1_, f32[16,128]{1,0:T(8,128)S(1)} %copy-done.5), custom_call_target="tpu_custom_call" | custom-call | tf_op jit(solution)/shard_map/pallas_call | solution.py:136
  40.6 0.7 copy-done.1
  41.8 1.0 %multiply_divide_fusion.sinv_ref.linv_ref = f32[512,1]{1,0:T(8,128)} fusion(f32[512,1]{1,0:T(8,128)S(1)} %copy.13.sscale_ref.lscale_ref), kind=kLoop, calls=%fused_computation.21 | loop fusion | flops 1024 | bytes 4096 | tf_op jit(solution)/shard_map/div | solution.py:270
  42.7 0.4 multiply_reduce_fusion.1
  43.2 3.1 %multiply_reduce_fusion = f32[2048]{0:T(1024)S(1)} fusion(bf16[2048,1024]{1,0:T(8,128)(2,1)} %cent_ref.1), kind=kLoop, calls=%fused_computation.1 | loop fusion | flops 6289408 | bytes 4202496 | tf_op jit(solution)/shard_map/reduce_sum | solution.py:23
  46.3 0.6 add_sqrt_fusion
  47.3 0.7 broadcast_multiply_fusion
  48.1 0.9 %copy-done.3 = f32[512,1]{1,0:T(8,128)S(1)} copy-done((f32[512,1]{1,0:T(8,128)S(1)}, f32[512,1]{1,0:T(8,128)}, u32[]{:S(2)}) %copy-start.3) | copy-done | bytes 2072
  49.0 18.5 %shard_map.88 = (f32[4,16,256]{2,1,0:T(8,128)S(1)}, f32[4,512,256]{2,1,0:T(8,128)S(1)}) custom-call(bf16[2048,1024]{1,0:T(8,128)(2,1)} %cent_ref.1, f32[2048,1]{1,0:T(8,128)S(1)} %copy.15.inv_ref, f32[16,2048]{1,0:T(8,128)S(1)} %pad.8.weight_ref, bf16[4,1024,256]{2,1,0:T(8,128)(2,1)} %copy-done, f32[4,1,256]{2,1,0:T(1,128)S(1)} %sqrt.57.bscale_ref, ...), custom_call_target="tpu_custom_call" | custom-call | tf_op jit(solution)/shard_map/pallas_call | solution.py:274
  67.5 16.2 %shard_map.89 = (f32[16,256]{1,0:T(8,128)S(1)}, f32[4,16,256]{2,1,0:T(8,128)S(1)}) custom-call(f32[4,16,256]{2,1,0:T(8,128)S(1)} %get-tuple-element.11.part_ref, f32[16,256]{1,0:T(8,128)S(1)} %pad.9.target_ref), custom_call_target="tpu_custom_call" | custom-call | tf_op jit(solution)/shard_map/pallas_call | solution.py:299
  83.8 0.5 fusion.6
  84.3 0.5 convolution_add_fusion.2
  84.8 0.5 convolution_add_fusion.1
  85.4 0.5 fusion.2
  86.5 1.6 %shard_map.90 = f32[512,512]{1,0:T(8,128)S(1)} custom-call(bf16[512,1024]{1,0:T(8,128)(2,1)S(1)} %bitcast.42, f32[512,1]{1,0:T(8,128)S(1)} %copy-done.3, f32[512,1]{1,0:T(8,128)S(1)} %copy.13.sscale_ref.lscale_ref, bf16[512,1024]{1,0:T(8,128)(2,1)S(1)} %bitcast.43, f32[1,512]{1,0:T(1,128)S(1)} %bitcast.49), custom_call_target="tpu_custom_call" | custom-call | tf_op jit(solution)/shard_map/pallas_call | solution.py:286
  88.1 0.6 fusion
  89.3 0.7 dynamic-slice_subtract_fusion
  89.9 0.6 copy.19
  (26 shorter events, 2.1 us)
Async XLA Ops:
  5.4 1.2 %copy-start.4 = (bf16[128,4096]{1,0:T(8,128)(2,1)S(1)}, bf16[128,4096]{1,0:T(8,128)(2,1)}, u32[]{:S(2)}) copy-start(bf16[128,4096]{1,0:T(8,128)(2,1)} %pool_ref.1) | copy-start | bytes 3145732
  7.1 0.7 copy-start.5
  40.6 0.7 copy-start.1
  41.3 5.0 %copy-start = (bf16[4,1024,256]{2,1,0:T(8,128)(2,1)}, bf16[4,1024,256]{2,1,0:T(8,128)(2,1)S(1)}, u32[]{:S(2)}) copy-start(bf16[4,1024,256]{2,1,0:T(8,128)(2,1)S(1)} %get-tuple-element.9.batch_ref) | copy-start | bytes 6291460
  43.2 4.1 %copy-start.6 = (f32[10,2048]{1,0:T(8,128)S(1)}, f32[10,2048]{1,0:T(8,128)}, u32[]{:S(2)}) copy-start(f32[10,2048]{1,0:T(8,128)} %param.11) | copy-start | bytes 245764
  48.0 1.0 %copy-start.3 = (f32[512,1]{1,0:T(8,128)S(1)}, f32[512,1]{1,0:T(8,128)}, u32[]{:S(2)}) copy-start(f32[512,1]{1,0:T(8,128)} %multiply_divide_fusion.sinv_ref.linv_ref) | copy-start | bytes 6148
  49.0 18.5 %copy-start.7 = (f32[10,256]{1,0:T(8,128)S(1)}, f32[10,256]{1,0:T(8,128)}, u32[]{:S(2)}) copy-start(f32[10,256]{1,0:T(8,128)} %param.9) | copy-start | bytes 30724
  67.5 18.4 %copy-start.2 = (f32[4,128,128]{2,1,0:T(8,128)S(1)}, f32[4,128,128]{2,1,0:T(8,128)}, u32[]{:S(2)}) copy-start(f32[4,128,128]{2,1,0:T(8,128)} %copy-done.1) | copy-start | bytes 786436

commit v2 on v1

--- a/solution.py
+++ b/solution.py
@@ -48,9 +48,14 @@
     out_ref[...] = total.astype(out_ref.dtype)
 
 
-def gather_kernel(groups, rows, count, *refs):
-    ins, outs = refs[:count], refs[count:2 * count]
-    (own, send1, recv1, send2, recv2, send3, recv3) = refs[2 * count:]
+def fused_kernel(groups, rows, count, tile, whole, *refs):
+    ins = refs[:count]
+    cent_ref, inv_ref, weight_ref = refs[count:count + 3]
+    refs = refs[count + 3:]
+    part_ref, cross_ref = refs[:2]
+    outs = (refs[count + 1],) + refs[2:count + 1]
+    (scales, own, send1, recv1, send2, recv2, send3, recv3) = refs[count + 2:]
+    width = cent_ref.shape[1]
     pairs = rows // 2
     c = lax.axis_index("centre")
     r = lax.axis_index("row")
@@ -94,51 +99,113 @@
         copy.start()
         sent.append(copy)
 
-    for a in range(count):
+    def here(a, d):
+        place = slot(a, r, (c + groups - d) % groups)
+        if d:
+            pltpu.make_async_remote_copy(
+                ins[a], place, send1.at[a, d], recv1.at[a, d],
+                device_id=(c, r), device_id_type=MESH).wait_recv()
+        for e in range(1, pairs):
+            copy = pltpu.make_async_remote_copy(
+                place, place, send2.at[a, e, d], recv2.at[a, e, d],
+                device_id=(c, ((x + e) % pairs) * 2 + core), device_id_type=MESH)
+            copy.start()
+            sent.append(copy)
+        forward(a, r, d, 0)
+
+    def across(a, e):
+        row = ((x + pairs - e) % pairs) * 2 + core
         for d in range(groups):
-            place = slot(a, r, (c + groups - d) % groups)
-            if d:
-                pltpu.make_async_remote_copy(
-                    ins[a], place, send1.at[a, d], recv1.at[a, d],
-                    device_id=(c, r), device_id_type=MESH).wait_recv()
-            for e in range(1, pairs):
-                copy = pltpu.make_async_remote_copy(
-                    place, place, send2.at[a, e, d], recv2.at[a, e, d],
-                    device_id=(c, ((x + e) % pairs) * 2 + core), device_id_type=MESH)
-                copy.start()
-                sent.append(copy)
-            forward(a, r, d, 0)
-    for a in range(count):
+            place = slot(a, row, (c + groups - d) % groups)
+            pltpu.make_async_remote_copy(
+                place, place, send2.at[a, e, d], recv2.at[a, e, d],
+                device_id=(c, r), device_id_type=MESH).wait_recv()
+            forward(a, row, d, e)
+        return row
+
+    def paired(a, e):
+        row = ((x + pairs - e) % pairs) * 2 + (1 - core)
         for d in range(groups):
-            for e in range(1, pairs):
-                row = ((x + pairs - e) % pairs) * 2 + core
-                place = slot(a, row, (c + groups - d) % groups)
-                pltpu.make_async_remote_copy(
-                    place, place, send2.at[a, e, d], recv2.at[a, e, d],
-                    device_id=(c, r), device_id_type=MESH).wait_recv()
-                forward(a, row, d, e)
-    for a in range(count):
+            place = slot(a, row, (c + groups - d) % groups)
+            pltpu.make_async_remote_copy(
+                place, place, send3.at[a, e, d], recv3.at[a, e, d],
+                device_id=(c, r), device_id_type=MESH).wait_recv()
+        return row
+
+    def block(row):
+        batch = outs[0][row]
+        exact = batch.astype(jnp.float32)
+        bscale = jnp.sqrt(jnp.mean(exact * exact, axis=0, keepdims=True) + EPS)
+        scales[row] = bscale
+        binv = 1.0 / bscale
+        half = weight_ref.shape[0]
+        first = jnp.zeros((2 * half, batch.shape[1]), jnp.float32)
+        second = jnp.zeros((half, batch.shape[1]), jnp.float32)
+        for start in range(0, cent_ref.shape[0], tile):
+            inner = jnp.dot(cent_ref[start:start + tile, :], batch, preferred_element_type=jnp.float32)
+            value = arc(inner * inv_ref[start:start + tile, :] * binv)
+            high = value.astype(jnp.bfloat16)
+            low = (value - high.astype(jnp.float32)).astype(jnp.bfloat16)
+            full = weight_ref[:, start:start + tile]
+            upper = full.astype(jnp.bfloat16)
+            lower = (full - upper.astype(jnp.float32)).astype(jnp.bfloat16)
+            coeffs = jnp.concatenate([upper, lower], axis=0)
+            first += jnp.dot(coeffs, high, preferred_element_type=jnp.float32)
+            second += jnp.dot(upper, low, preferred_element_type=jnp.float32)
+        part_ref[row] = (first[:half] + (first[half:] + second)) * bscale
+
+    later = range(1, count)
+    for d in range(groups):
+        here(0, d)
+    block(r)
+    for a in later:
         for d in range(groups):
-            for e in range(pairs):
-                row = ((x + pairs - e) % pairs) * 2 + (1 - core)
-                place = slot(a, row, (c + groups - d) % groups)
-                pltpu.make_async_remote_copy(
-                    place, place, send3.at[a, e, d], recv3.at[a, e, d],
-                    device_id=(c, r), device_id_type=MESH).wait_recv()
+            here(a, d)
+    block(paired(0, 0))
+    for e in range(1, pairs):
+        row = across(0, e)
+        block(row)
+        if e == pairs - 1:
+            for a in later:
+                paired(a, 0)
+                for f in range(1, pairs):
+                    across(a, f)
+        block(paired(0, e))
+    for a in later:
+        for e in range(1, pairs):
+            paired(a, e)
+
+    for part in range(rows if whole else 1):
+        left = outs[1][part] if whole else ins[1][...]
+        exact = left.astype(jnp.float32)
+        lscale = jnp.sqrt(jnp.mean(exact * exact, axis=1, keepdims=True) + EPS)
+        linv = 1.0 / (width * lscale)
+        size = left.shape[0]
+        for row in range(rows):
+            bscale = scales[row]
+            inner = jnp.dot(left, outs[0][row], preferred_element_type=jnp.float32)
+            value = arc(inner * linv * (1.0 / bscale))
+            cross_ref[row, part * size:(part + 1) * size, :] = value * (lscale * bscale)
     for copy in sent:
         copy.wait_send()
 
 
-def gather_all(groups, rows, arrays):
+def fused(groups, rows, arrays, centres, inv, scaled, whole):
     count = len(arrays)
     pairs = rows // 2
     dma = pltpu.SemaphoreType.DMA
+    cols = arrays[0].shape[1]
+    extra = arrays[1].shape[0] * (groups * rows if whole else 1)
+    spread = [jax.ShapeDtypeStruct((rows, groups * a.shape[0], a.shape[1]), a.dtype) for a in arrays]
     return pl.pallas_call(
-        functools.partial(gather_kernel, groups, rows, count),
-        out_shape=[jax.ShapeDtypeStruct((rows, groups * a.shape[0], a.shape[1]), a.dtype) for a in arrays],
-        in_specs=[VMEM] * count,
-        out_specs=[VMEM] * count,
+        functools.partial(fused_kernel, groups, rows, count, 512, whole),
+        out_shape=[jax.ShapeDtypeStruct((rows, scaled.shape[0], cols), jnp.float32),
+                   jax.ShapeDtypeStruct((rows, extra, cols), jnp.float32)] + spread[1:],
+        in_specs=[VMEM] * (count + 3),
+        out_specs=[VMEM] * (count + 1),
         scratch_shapes=[
+            pltpu.VMEM(spread[0].shape, spread[0].dtype),
+            pltpu.VMEM((rows, 1, cols), jnp.float32),
             dma((count,)),
             dma((count, groups)), dma((count, groups)),
             dma((count, pairs, groups)), dma((count, pairs, groups)),
@@ -146,35 +213,7 @@
         ],
         compiler_params=pltpu.CompilerParams(
             collective_id=0, has_side_effects=True, vmem_limit_bytes=48 << 20),
-    )(*arrays)
-
-
-def main_kernel(tile, cent_ref, inv_ref, weight_ref, batch_ref, bscale_ref, samp_ref, sinv_ref, sscale_ref,
-                part_ref, cross_ref):
-    bscale = bscale_ref[0]
-    binv = 1.0 / bscale
-    batch = batch_ref[0]
-    half = weight_ref.shape[0]
-    first = jnp.zeros((2 * half, batch.shape[1]), jnp.float32)
-    second = jnp.zeros((half, batch.shape[1]), jnp.float32)
-    for start in range(0, cent_ref.shape[0], tile):
-        inner = jnp.dot(cent_ref[start:start + tile, :], batch, preferred_element_type=jnp.float32)
-        value = arc(inner * inv_ref[start:start + tile, :] * binv)
-        high = value.astype(jnp.bfloat16)
-        low = (value - high.astype(jnp.float32)).astype(jnp.bfloat16)
-        exact = weight_ref[:, start:start + tile]
-        upper = exact.astype(jnp.bfloat16)
-        lower = (exact - upper.astype(jnp.float32)).astype(jnp.bfloat16)
-        coeffs = jnp.concatenate([upper, lower], axis=0)
-        first += jnp.dot(coeffs, high, preferred_element_type=jnp.float32)
-        second += jnp.dot(upper, low, preferred_element_type=jnp.float32)
-    part_ref[0] = (first[:half] + (first[half:] + second)) * bscale
-    count = samp_ref.shape[0]
-    step = min(tile, count)
-    for start in range(0, count, step):
-        inner = jnp.dot(samp_ref[start:start + step, :], batch, preferred_element_type=jnp.float32)
-        value = arc(inner * sinv_ref[start:start + step, :] * binv)
-        cross_ref[0, start:start + step, :] = value * (sscale_ref[start:start + step, :] * bscale)
+    )(*arrays, centres, inv, scaled)
 
 
 def gram_kernel(left_ref, linv_ref, lscale_ref, right_ref, rscale_ref, out_ref):
@@ -256,32 +295,17 @@
     local_sample = sample_index - lax.axis_index(("centre", "row")) * cent_dev
     sample_rows = jnp.take(centres, local_sample, axis=0)
     arrays = [picked, sample_rows] + ([factor] if whole else [])
-    gathered = gather_all(groups, rows, arrays)
-    batch = gathered[0]
-    samples = gathered[1].reshape(total_samp, -1)
-
     centre_scale = row_scale(centres, 1)
     scaled = jnp.pad(weights * centre_scale[None, :], ((0, half - labels), (0, 0)))
     inv = (1.0 / (width * centre_scale))[:, None]
-    bscale = row_scale(batch, 1)[:, None, :]
+    partial, cross, *gathered = fused(groups, rows, arrays, centres, inv, scaled, whole)
+    samples = gathered[0].reshape(total_samp, -1)
     sscale = row_scale(samples, 1)
     left = samples if whole else sample_rows
     lscale = (sscale if whole else row_scale(sample_rows, 1))[:, None]
     linv = 1.0 / (width * lscale)
     extra = left.shape[0]
     fixed = lambda shape: pl.BlockSpec(shape, lambda i: (0, 0))
-    moving = lambda a, b: pl.BlockSpec((1, a, b), lambda i: (i, 0, 0))
-    partial, cross = pl.pallas_call(
-        functools.partial(main_kernel, 256),
-        grid=(rows,),
-        out_shape=[jax.ShapeDtypeStruct((rows, half, rows_dev), jnp.float32),
-                   jax.ShapeDtypeStruct((rows, extra, rows_dev), jnp.float32)],
-        in_specs=[fixed(centres.shape), fixed(inv.shape), fixed(scaled.shape),
-                  moving(batch.shape[1], rows_dev), moving(1, rows_dev),
-                  fixed(left.shape), fixed(linv.shape), fixed(lscale.shape)],
-        out_specs=[moving(half, rows_dev), moving(extra, rows_dev)],
-        compiler_params=params,
-    )(centres, inv, scaled, batch, bscale, left, linv, lscale)
     tile = min(512, total_samp)
     gram = pl.pallas_call(
         gram_kernel,
@@ -318,7 +342,7 @@
 
     push = sum(lax.dot_general(grad_all[i], cross[i], CONTRACT, precision=HIGH) for i in range(rows)) / total_rows
     if whole:
-        factors = gathered[2].reshape(total_samp, -1)
+        factors = gathered[1].reshape(total_samp, -1)
         update = jnp.zeros_like(push)
         for step in range(PROJ_STEPS):
             slope = push if step == 0 else times(update, gram) / total_samp + push

time: 90.9 us -> 75.5 us (0.83)
  Pallas kernels: 69.6 us -> 59.2 us
  other arithmetic: 8.23 us -> 5.6 us
  local copies, waits for them, and re-layouts: 8.06 us -> 5.73 us
    pallas_call x2 -> x1, Pallas kernels: 51.3 us -> 42.8 us  [fused(): pl.pallas_call(functools.partial(fused_kernel, groups, rows, count, 512,...]
    unnamed x17 -> x9, local copies, waits for them, and re-layouts: 4.18 us -> 1.84 us
    pallas_call x1, Pallas kernels: 16.2 us -> 14.5 us  [on_device(): pl.pallas_call(functools.partial(sum_kernel, groups, rows), out_shape=[ja...]
    reduce_sum x3 -> x2, other arithmetic: 3.81 us -> 3.4 us  [row_scale(): return jnp.sqrt(jnp.mean(values * values, axis=axis) + EPS)]
where the time goes in v2:
time: 75.5 us; the launch traced here: 75.2 us
  Pallas kernels  59.2 us (78%)
  local copies, waits for them, and re-layouts  5.73 us (8%)
  other arithmetic  5.6 us (7%)
  matrix products  3.85 us (5%)
  between operations  0.83 us (1%)
    pallas_call x1, Pallas kernels, fused(): pl.pallas_call(functools.partial(fused_kernel, groups, rows, count, 512,...  42.8 us
    pallas_call x1, Pallas kernels, on_device(): pl.pallas_call(functools.partial(sum_kernel, groups, rows), out_shape=[ja...  14.5 us
    reduce_sum x2, other arithmetic, row_scale(): return jnp.sqrt(jnp.mean(values * values, axis=axis) + EPS)  3.4 us
    gather x1, local copies, waits for them, and re-layouts, on_device(): sample_rows = jnp.take(centres, local_sample, axis=0)  3.34 us
    dot_general x4, matrix products, on_device(): lax.dot_general(grad_all[i], cross[i], CONTRACT, precision=HIGH)  2.11 us
    unnamed x9, local copies, waits for them, and re-layouts  1.84 us
    pallas_call x1, Pallas kernels, on_device(): pl.pallas_call(gram_kernel, grid=(total_samp // tile,), out_shape=jax.Sha...  1.57 us

profile of v2, /device:TPU:0, one launch (start us, length us, event | category | flops | bytes accessed | tf_op | source)
XLA Modules:
  0.0 75.2 jit_solution(14659258046540870075)
XLA Ops:
  0.6 0.7 broadcast_subtract_fusion
  1.3 1.2 %copy-done = bf16[128,4096]{1,0:T(8,128)(2,1)S(1)} copy-done((bf16[128,4096]{1,0:T(8,128)(2,1)S(1)}, bf16[128,4096]{1,0:T(8,128)(2,1)}, u32[]{:S(2)}) %copy-start) | copy-done | bytes 1048600
  2.5 0.4 shard_map.86.refs_0_
  3.0 0.7 compare_and_fusion
  3.7 3.3 %gather_fusion = bf16[16,1024]{1,0:T(8,128)(2,1)S(1)} fusion(bf16[2048,1024]{1,0:T(8,128)(2,1)} %refs_3_.1, s32[1024]{0:T(1024)S(1)} %pad_clamp_fusion), kind=kCustom, calls=%fused_computation | custom fusion | bytes 65600 | tf_op jit(solution)/shard_map/jit(_take)/gather | solution.py:296
  7.0 0.1 broadcast_select_fusion.refs_1_
  7.1 3.1 %multiply_reduce_fusion = f32[2048]{0:T(1024)S(1)} fusion(bf16[2048,1024]{1,0:T(8,128)(2,1)} %refs_3_.1), kind=kLoop, calls=%fused_computation.1 | loop fusion | flops 6289408 | bytes 4202496 | tf_op jit(solution)/shard_map/reduce_sum | solution.py:23
  10.2 0.4 copy.12.refs_4_
  10.7 42.8 %shard_map.87 = (f32[4,16,256]{2,1,0:T(8,128)S(1)}, f32[4,512,256]{2,1,0:T(8,128)S(1)}, bf16[4,128,1024]{2,1,0:T(8,128)(2,1)S(1)}, f32[4,128,128]{2,1,0:T(8,128)S(1)}) custom-call(bf16[128,256]{1,0:T(8,128)(2,1)S(1)} %shard_map.86.refs_0_, bf16[16,1024]{1,0:T(8,128)(2,1)S(1)} %broadcast_select_fusion.refs_1_, f32[16,128]{1,0:T(8,128)S(1)} %copy-done.1, ...), custom_call_target="tpu_custom_call" | custom-call | tf_op jit(solution)/shard_map/pallas_call | solution.py:200
  53.5 14.5 %shard_map.88 = (f32[16,256]{1,0:T(8,128)S(1)}, f32[4,16,256]{2,1,0:T(8,128)S(1)}) custom-call(f32[4,16,256]{2,1,0:T(8,128)S(1)} %get-tuple-element.8.part_ref, f32[16,256]{1,0:T(8,128)S(1)} %pad.9.target_ref), custom_call_target="tpu_custom_call" | custom-call | tf_op jit(solution)/shard_map/pallas_call | solution.py:323
  68.0 0.5 fusion.6
  68.5 0.5 convolution_add_fusion.2
  69.0 0.5 convolution_add_fusion.1
  69.6 0.5 fusion.2
  70.1 0.2 fusion.20
  70.4 0.3 fusion.1
  70.7 0.3 multiply_reduce_fusion.1
  71.0 0.2 copy.13.lscale_ref
  71.2 1.6 %shard_map.89 = f32[512,512]{1,0:T(8,128)S(1)} custom-call(bf16[512,1024]{1,0:T(8,128)(2,1)S(1)} %bitcast.41, f32[512,1]{1,0:T(8,128)S(1)} %multiply_divide_fusion.linv_ref, f32[512,1]{1,0:T(8,128)S(1)} %copy.13.lscale_ref, bf16[512,1024]{1,0:T(8,128)(2,1)S(1)} %bitcast.42, f32[1,512]{1,0:T(1,128)S(1)} %bitcast.48), custom_call_target="tpu_custom_call" | custom-call | tf_op jit(solution)/shard_map/pallas_call | solution.py:310
  72.8 0.6 fusion
  73.4 0.2 fusion.21
  73.6 0.3 fusion.22
  74.0 0.7 dynamic-slice_subtract_fusion
  74.6 0.6 copy.17
  (14 shorter events, 0.1 us)
Async XLA Ops:
  1.3 1.2 %copy-start = (bf16[128,4096]{1,0:T(8,128)(2,1)S(1)}, bf16[128,4096]{1,0:T(8,128)(2,1)}, u32[]{:S(2)}) copy-start(bf16[128,4096]{1,0:T(8,128)(2,1)} %pool_ref.1) | copy-start | bytes 3145732
  7.1 3.5 %copy-start.2 = (f32[10,2048]{1,0:T(8,128)S(1)}, f32[10,2048]{1,0:T(8,128)}, u32[]{:S(2)}) copy-start(f32[10,2048]{1,0:T(8,128)} %param.11) | copy-start | bytes 245764
  7.1 3.6 %copy-start.1 = (f32[16,128]{1,0:T(8,128)S(1)}, f32[16,128]{1,0:T(8,128)}, u32[]{:S(2)}) copy-start(f32[16,128]{1,0:T(8,128)} %refs_2_.1) | copy-start | bytes 24580
  10.7 42.8 %copy-start.3 = (f32[10,256]{1,0:T(8,128)S(1)}, f32[10,256]{1,0:T(8,128)}, u32[]{:S(2)}) copy-start(f32[10,256]{1,0:T(8,128)} %param.9) | copy-start | bytes 30724

commit v3 on v2

--- a/solution.py
+++ b/solution.py
@@ -14,8 +14,8 @@
 MESH = pl.DeviceIdType.MESH
 CONTRACT = (((1,), (1,)), ((), ()))
 VMEM = pl.BlockSpec(memory_space=pltpu.VMEM)
-POLY = (0.3183098802, -0.8408441305, 0.09680761083, -0.03656900053,
-        0.01880055716, -0.00968401399, 0.003746990699, -0.0007261497719)
+POLY = (0.3183098418, -0.8408396621, 0.09672484892, -0.03600487561,
+        0.01699589254, -0.006754446989, 0.00141088352)
 
 
 def row_scale(rows, axis):
@@ -46,6 +46,22 @@
         total += jnp.dot(pool_ref[:, start:start + size], hot.astype(jnp.bfloat16),
                          preferred_element_type=jnp.float32)
     out_ref[...] = total.astype(out_ref.dtype)
+
+
+def rows_kernel(cent_ref, index_ref, out_ref, scale_ref):
+    step = pl.program_id(0)
+    tile = cent_ref.shape[0]
+    rows = cent_ref[...]
+    hot = lax.broadcasted_iota(jnp.int32, (index_ref.shape[0], tile), 1) + step * tile == index_ref[...]
+    found = jnp.dot(hot.astype(jnp.bfloat16), rows, preferred_element_type=jnp.float32)
+
+    @pl.when(step == 0)
+    def _():
+        out_ref[...] = jnp.zeros_like(out_ref)
+
+    out_ref[...] = (out_ref[...].astype(jnp.float32) + found).astype(out_ref.dtype)
+    exact = rows.astype(jnp.float32)
+    scale_ref[...] = jnp.sqrt(jnp.mean(exact * exact, axis=1, keepdims=True) + EPS)
 
 
 def fused_kernel(groups, rows, count, tile, whole, *refs):
@@ -293,11 +309,20 @@
         compiler_params=params,
     )(pool, local_batch[None, :])
     local_sample = sample_index - lax.axis_index(("centre", "row")) * cent_dev
-    sample_rows = jnp.take(centres, local_sample, axis=0)
+    sample_rows, centre_scale = pl.pallas_call(
+        rows_kernel,
+        grid=(cent_dev // 512,),
+        out_shape=[jax.ShapeDtypeStruct((samp_dev, centres.shape[1]), centres.dtype),
+                   jax.ShapeDtypeStruct((cent_dev, 1), jnp.float32)],
+        in_specs=[pl.BlockSpec((512, centres.shape[1]), lambda i: (i, 0)),
+                  pl.BlockSpec((samp_dev, 1), lambda i: (0, 0))],
+        out_specs=[pl.BlockSpec((samp_dev, centres.shape[1]), lambda i: (0, 0)),
+                   pl.BlockSpec((512, 1), lambda i: (i, 0))],
+        compiler_params=params,
+    )(centres, local_sample[:, None])
     arrays = [picked, sample_rows] + ([factor] if whole else [])
-    centre_scale = row_scale(centres, 1)
-    scaled = jnp.pad(weights * centre_scale[None, :], ((0, half - labels), (0, 0)))
-    inv = (1.0 / (width * centre_scale))[:, None]
+    scaled = jnp.pad(weights * centre_scale.T, ((0, half - labels), (0, 0)))
+    inv = 1.0 / (width * centre_scale)
     partial, cross, *gathered = fused(groups, rows, arrays, centres, inv, scaled, whole)
     samples = gathered[0].reshape(total_samp, -1)
     sscale = row_scale(samples, 1)

time: 75.5 us -> 73.6 us (0.975)
  other arithmetic: 5.6 us -> 2.73 us
  Pallas kernels: 59.2 us -> 61.1 us
  local copies, waits for them, and re-layouts: 5.73 us -> 4.82 us
    gather x1 -> x0, local copies, waits for them, and re-layouts: 3.34 us -> none  [on_device(): sample_rows = jnp.take(centres, local_sample, axis=0)]
    reduce_sum x2 -> x1, other arithmetic: 3.4 us -> 0.29 us  [row_scale(): return jnp.sqrt(jnp.mean(values * values, axis=axis) + EPS)]
    unnamed x9 -> x11, local copies, waits for them, and re-layouts: 1.84 us -> 4.56 us
    pallas_call x0 -> x1, Pallas kernels: none -> 2.31 us  [on_device(): pl.pallas_call(rows_kernel, grid=(cent_dev // 512,), out_shape=[jax.Shape...]
where the time goes in v3:
time: 73.6 us; the launch traced here: 73.3 us
  Pallas kernels  61.1 us (83%)
  local copies, waits for them, and re-layouts  4.82 us (7%)
  matrix products  3.85 us (5%)
  other arithmetic  2.73 us (4%)
  between operations  0.82 us (1%)
    pallas_call x1, Pallas kernels, fused(): pl.pallas_call(functools.partial(fused_kernel, groups, rows, count, 512,...  42.2 us
    pallas_call x1, Pallas kernels, on_device(): pl.pallas_call(functools.partial(sum_kernel, groups, rows), out_shape=[ja...  14.6 us
    unnamed x11, local copies, waits for them, and re-layouts  4.56 us
    pallas_call x1, Pallas kernels, on_device(): pl.pallas_call(rows_kernel, grid=(cent_dev // 512,), out_shape=[jax.Shape...  2.31 us
    dot_general x4, matrix products, on_device(): lax.dot_general(grad_all[i], cross[i], CONTRACT, precision=HIGH)  2.11 us
    pallas_call x1, Pallas kernels, on_device(): pl.pallas_call(gram_kernel, grid=(total_samp // tile,), out_shape=jax.Sha...  1.49 us

profile of v3, /device:TPU:0, one launch (start us, length us, event | category | flops | bytes accessed | tf_op | source)
XLA Modules:
  0.0 73.3 jit_solution(5579259067769329821)
XLA Ops:
  0.6 0.7 broadcast_subtract_fusion
  1.3 1.2 %copy-done.1 = bf16[128,4096]{1,0:T(8,128)(2,1)S(1)} copy-done((bf16[128,4096]{1,0:T(8,128)(2,1)S(1)}, bf16[128,4096]{1,0:T(8,128)(2,1)}, u32[]{:S(2)}) %copy-start.1) | copy-done | bytes 1048600
  2.5 0.4 shard_map.86.refs_0_
  3.0 0.7 subtract_bitcast_fusion
  3.8 2.2 %copy-done = bf16[2048,1024]{1,0:T(8,128)(2,1)S(1)} copy-done((bf16[2048,1024]{1,0:T(8,128)(2,1)S(1)}, bf16[2048,1024]{1,0:T(8,128)(2,1)}, u32[]{:S(2)}) %copy-start) | copy-done | bytes 4194328
  5.9 2.3 %shard_map.87 = (bf16[16,1024]{1,0:T(8,128)(2,1)S(1)}, f32[2048,1]{1,0:T(8,128)S(1)}) custom-call(bf16[2048,1024]{1,0:T(8,128)(2,1)S(1)} %copy-done, s32[16,1]{1,0:T(8,128)S(1)} %copy.13.index_ref), custom_call_target="tpu_custom_call" | custom-call | tf_op jit(solution)/shard_map/pallas_call | solution.py:312
  8.3 0.3 fusion.20
  8.6 0.5 copy-done.3
  9.2 42.2 %shard_map.88 = (f32[4,16,256]{2,1,0:T(8,128)S(1)}, f32[4,512,256]{2,1,0:T(8,128)S(1)}, bf16[4,128,1024]{2,1,0:T(8,128)(2,1)S(1)}, f32[4,128,128]{2,1,0:T(8,128)S(1)}) custom-call(bf16[128,256]{1,0:T(8,128)(2,1)S(1)} %shard_map.86.refs_0_, bf16[16,1024]{1,0:T(8,128)(2,1)S(1)} %get-tuple-element.10.refs_1_, f32[16,128]{1,0:T(8,128)S(1)} %copy-done.2, ...), custom_call_target="tpu_custom_call" | custom-call | tf_op jit(solution)/shard_map/pallas_call | solution.py:216
  51.5 14.6 %shard_map.89 = (f32[16,256]{1,0:T(8,128)S(1)}, f32[4,16,256]{2,1,0:T(8,128)S(1)}) custom-call(f32[4,16,256]{2,1,0:T(8,128)S(1)} %get-tuple-element.12.part_ref, f32[16,256]{1,0:T(8,128)S(1)} %pad.9.target_ref), custom_call_target="tpu_custom_call" | custom-call | tf_op jit(solution)/shard_map/pallas_call | solution.py:348
  66.1 0.5 fusion.6
  66.6 0.5 convolution_add_fusion.2
  67.2 0.5 convolution_add_fusion.1
  67.7 0.5 fusion.2
  68.2 0.2 fusion.21
  68.5 0.3 fusion.1
  68.8 0.3 multiply_reduce_fusion
  69.1 0.2 copy.14.lscale_ref
  69.3 1.5 %shard_map.90 = f32[512,512]{1,0:T(8,128)S(1)} custom-call(bf16[512,1024]{1,0:T(8,128)(2,1)S(1)} %bitcast.42, f32[512,1]{1,0:T(8,128)S(1)} %multiply_divide_fusion.1.linv_ref, f32[512,1]{1,0:T(8,128)S(1)} %copy.14.lscale_ref, bf16[512,1024]{1,0:T(8,128)(2,1)S(1)} %bitcast.43, f32[1,512]{1,0:T(1,128)S(1)} %bitcast.49), custom_call_target="tpu_custom_call" | custom-call | tf_op jit(solution)/shard_map/pallas_call | solution.py:335
  70.8 0.6 fusion
  71.4 0.2 fusion.22
  71.7 0.3 fusion.23
  72.0 0.7 dynamic-slice_subtract_fusion
  72.7 0.6 copy.18
  (13 shorter events, 0.2 us)
Async XLA Ops:
  1.3 1.2 %copy-start.1 = (bf16[128,4096]{1,0:T(8,128)(2,1)S(1)}, bf16[128,4096]{1,0:T(8,128)(2,1)}, u32[]{:S(2)}) copy-start(bf16[128,4096]{1,0:T(8,128)(2,1)} %pool_ref.1) | copy-start | bytes 3145732
  3.8 2.2 %copy-start = (bf16[2048,1024]{1,0:T(8,128)(2,1)S(1)}, bf16[2048,1024]{1,0:T(8,128)(2,1)}, u32[]{:S(2)}) copy-start(bf16[2048,1024]{1,0:T(8,128)(2,1)} %refs_3_.1) | copy-start | bytes 12582916
  8.3 0.9 %copy-start.3 = (f32[10,2048]{1,0:T(8,128)S(1)}, f32[10,2048]{1,0:T(8,128)}, u32[]{:S(2)}) copy-start(f32[10,2048]{1,0:T(8,128)} %param.11) | copy-start | bytes 245764
  8.3 0.9 %copy-start.2 = (f32[16,128]{1,0:T(8,128)S(1)}, f32[16,128]{1,0:T(8,128)}, u32[]{:S(2)}) copy-start(f32[16,128]{1,0:T(8,128)} %refs_2_.1) | copy-start | bytes 24580
  9.2 42.3 %copy-start.4 = (f32[10,256]{1,0:T(8,128)S(1)}, f32[10,256]{1,0:T(8,128)}, u32[]{:S(2)}) copy-start(f32[10,256]{1,0:T(8,128)} %param.9) | copy-start | bytes 30724
